TPU v7x, 32 devices: a whole 2x2x4 slice. The times are simulated.
32 devices in a mesh: group: 2 (over x), space: 16 (over z, y, core).
Axes of the slice: x: 2, y: 2, z: 4, core: 2. Of those that a mesh axis runs over, the one named last changes fastest.
Arguments:
- columns_in: bfloat16 [8192, 1024], P(('group', 'space')), parts along dimension 0, may hold values from -6 to 6
- cotangent: bfloat16 [8192, 1024], P(('group', 'space')), parts along dimension 0, may hold values from -6 to 6
- conv_weight: bfloat16 [7, 16, 16], replicated, may hold values from -0.5 to 0.5
- mix_weight: bfloat16 [1024, 1024], replicated, may hold values from -0.1875 to 0.1875
- neighbours: int32 [4096, 7], P('space'), may hold values from 0 to 4095, as said below
- rotations: int32 [4096], P('space'), may hold values from 0 to 5
- pentagons: int32 [4096], P('space'), may hold values 0 or 1
Outputs:
- grad_input: bfloat16 [8192, 1024], P(('group', 'space')), parts along dimension 0
- grad_mix: float32 [1024, 2048], P('space', 'group'), parts along dimension 1
- grad_conv: float32 [14, 16, 16], P('group'), parts along dimension 0
There are 2 independent parts, one for each index of `group`. A program takes and returns all parts, laid end to end along the dimension named above; an argument that names none is the same for every part. Nothing has to cross between parts.
Inputs may be any that keep to these rules, and one draw needn't show every extreme that they name: `neighbours`: entry 0 of each row is the column itself. Every other entry lies in the column's own grid row of 256 consecutive column indices or in the row just before or after it, the last row of the grid followed by the first. The relation is symmetric: if b is a neighbour of a, then a is a neighbour of b.
All inputs are finite; a program needn't handle non-finite values. No bound on the sum of `pentagons` on one device may be relied on, other than what follows from the above.
Results may differ from a plain program's by a relative error of at most 0.005.
Values may be sent and summed in bfloat16 or wider, within the bound.
A program may use at most 128 MiB of HBM per device.

v0:
```python
import jax
import jax.numpy as jnp
from jax import lax
from jax.sharding import PartitionSpec as P

ROW = 256


def with_halo(block, sides, width):
    for axis, dim in sides:
        count = lax.axis_size(axis)
        forward = [(i, i + 1) for i in range(count - 1)]
        forward.append((count - 1, 0))
        backward = [(target, source) for source, target in forward]
        low = lax.ppermute(
            lax.slice_in_dim(block, block.shape[dim] - width, None, axis=dim), axis, forward
        )
        high = lax.ppermute(lax.slice_in_dim(block, 0, width, axis=dim), axis, backward)
        block = jnp.concatenate([low, block, high], axis=dim)
    return block


def shifted(shard, axis, by):
    devices = lax.axis_size(axis)
    return lax.ppermute(shard, axis, [(i, (i + by) % devices) for i in range(devices)])


def shards(columns_in, cotangent, conv_weight, mix_weight, neighbours, rotations, pentagons):
    tile_cols = columns_in.shape[0]
    feature_width = columns_in.shape[1]
    channels = conv_weight.shape[1]
    lane_width = min(128, feature_width)
    blocks = lane_width // channels
    flat_rows = tile_cols * feature_width // lane_width
    devices = lax.axis_size("space")
    offset = lax.axis_index("space") * tile_cols
    total_cols = tile_cols * devices
    levels = feature_width // channels
    identity_block = jnp.eye(blocks, dtype=jnp.bfloat16)
    wide_weights = [
        jnp.kron(identity_block, conv_weight[index_tap])
        for index_tap in range(conv_weight.shape[0])
    ]
    extended = with_halo(columns_in, (("space", 0),), ROW)
    gathered = []
    preact = jnp.zeros((flat_rows, lane_width), jnp.float32)
    for index_tap in range(conv_weight.shape[0]):
        if index_tap == 0:
            slot_index = jnp.zeros_like(rotations)
        else:
            slot_index = 1 + (index_tap - 1 - rotations) % 6
        source = jnp.take_along_axis(neighbours, slot_index[:, None], axis=1)[:, 0]
        keep_mask = 1 - pentagons * (slot_index == 6).astype(jnp.int32)
        local_index = (source - offset + ROW) % total_cols
        tap_rows = jnp.take(extended, local_index, axis=0) * keep_mask.astype(jnp.bfloat16)[:, None]
        tap_rows = tap_rows.reshape(flat_rows, lane_width)
        gathered.append((local_index, keep_mask, tap_rows))
        preact = preact + jnp.dot(
            tap_rows, wide_weights[index_tap], preferred_element_type=jnp.float32
        )
    output, pullback = jax.vjp(jax.nn.gelu, preact)
    active = output.reshape(tile_cols, feature_width).astype(jnp.bfloat16)
    upstream = lax.dot_general(
        cotangent, mix_weight, (((1,), (1,)), ((), ())), preferred_element_type=jnp.float32
    )
    grad_pre = pullback(upstream.reshape(flat_rows, lane_width))[0].astype(jnp.bfloat16)
    spread = jnp.zeros((tile_cols + 2 * ROW, feature_width), jnp.float32)
    conv_terms = []
    for index_tap in range(conv_weight.shape[0]):
        local_index, keep_mask, tap_rows = gathered[index_tap]
        block_product = lax.dot_general(
            tap_rows, grad_pre, (((0,), (0,)), ((), ())), preferred_element_type=jnp.float32
        )
        block_product = block_product.reshape(blocks, channels, blocks, channels)
        conv_terms.append(jnp.sum(jnp.diagonal(block_product, axis1=0, axis2=2), axis=-1))
        tap_term = lax.dot_general(
            grad_pre,
            wide_weights[index_tap],
            (((1,), (1,)), ((), ())),
            preferred_element_type=jnp.float32,
        ).reshape(tile_cols, feature_width)
        tap_term = tap_term * keep_mask.astype(jnp.float32)[:, None]
        spread = spread.at[local_index].add(tap_term)
    local_conv = jnp.stack(conv_terms)
    share_rows = feature_width // devices
    local_mix = lax.dot_general(
        active, cotangent, (((0,), (0,)), ((), ())), preferred_element_type=jnp.float32
    )
    mix_total, conv_total = lax.psum((local_mix, local_conv), "space")
    mix_owned = lax.dynamic_slice_in_dim(
        mix_total, lax.axis_index("space") * share_rows, share_rows, 0
    )
    grad_mix = mix_owned / jnp.sqrt(jnp.float32(total_cols))
    grad_conv = conv_total / jnp.sqrt(jnp.float32(total_cols * levels))
    from_previous = shifted(spread[tile_cols + ROW :].astype(jnp.bfloat16), "space", 1).astype(
        jnp.float32
    )
    from_following = shifted(spread[:ROW].astype(jnp.bfloat16), "space", -1).astype(jnp.float32)
    inner = spread[ROW : ROW + tile_cols] + cotangent.astype(jnp.float32)
    inner = inner.at[:ROW].add(from_previous)
    inner = inner.at[tile_cols - ROW :].add(from_following)
    return (inner.astype(jnp.bfloat16), grad_mix, grad_conv)


def solution(mesh):
    return jax.shard_map(
        shards,
        mesh=mesh,
        in_specs=(
            P(("group", "space"), None),
            P(("group", "space"), None),
            P(),
            P(),
            P("space", None),
            P("space"),
            P("space"),
        ),
        out_specs=(P(("group", "space"), None), P("space", "group"), P("group", None, None)),
        check_vma=False,
    )
```

profile of v0, /device:TPU:0, one launch (start us, length us, event | category | flops | bytes accessed | tf_op | source)
XLA Modules:
  0.0 296.2 jit_solution(8525426926201532051)
XLA Ops:
  7.7 5.1 %collective-permute-start.1 = (bf16[256,1024]{1,0:T(8,128)(2,1)}, bf16[256,1024]{1,0:T(8,128)(2,1)}, u32[]{:S(2)}, u32[]{:S(2)}) collective-permute-start(bf16[256,1024]{1,0:T(8,128)(2,1)} %param.19), channel_id=1, source_target_pairs={{1,0},{2,1},{3,2},{4,3},{5,4},{6,5},{7,6},{8,7},{9,8},{10,9},{11,1... | collective-permute-start | bytes 1572872 | tf_op jit(solution)/shard_map/ppermute | solution.py:18
  13.7 2.3 gather_fusion.9
  17.4 2.3 gather_fusion.7
  29.9 2.0 gather_fusion.19
  44.3 2.1 reshape.307
  49.7 2.0 gather_fusion.14
  51.7 2.0 select_multiply_fusion.3
  53.7 2.1 reshape.310
  55.7 2.0 gather_fusion.16
  57.7 2.0 select_multiply_fusion.2
  59.7 2.1 reshape.311
  63.7 2.0 select_multiply_fusion.1
  65.7 2.0 reshape.312
  75.1 2.0 multiply_convert_fusion
  88.4 2.7 convolution_bitcast_fusion.5
  103.8 2.7 convolution_bitcast_fusion.1
  110.3 2.5 reshape.315
  112.8 2.4 reshape.316
  120.3 5.2 %scatter_custom_fusion = f32[768,1024]{1,0:T(8,128)} fusion(s32[256]{0:T(256)} %bitcast.267, f32[256,1024]{1,0:T(8,128)} %reshape.485, f32[]{:T(128)} %constant.220.clone.1), kind=kCustom, calls=%fused_computation.34 | custom fusion | flops 262144 | bytes 3146240 | tf_op jit(solution)/shard_map/scatter-add | solution.py:83
  125.5 7.4 %scatter_custom_fusion.1 = f32[768,1024]{1,0:T(8,128)} fusion(f32[768,1024]{1,0:T(8,128)} %scatter_custom_fusion, s32[256]{0:T(256)} %bitcast.268, f32[256,1024]{1,0:T(8,128)} %reshape.315, f32[256]{0:T(256)S(1)} %get-tuple-element.103), kind=kCustom, calls=%fused_computation.67 | custom fusion | flops 524288 | bytes 4195328 | tf_op jit(solution)/shard_map/scatter-add | solution.py:83
  132.9 7.0 %scatter_custom_fusion.2 = f32[768,1024]{1,0:T(8,128)} fusion(f32[768,1024]{1,0:T(8,128)} %scatter_custom_fusion.1, s32[256]{0:T(256)} %bitcast.269, f32[256,1024]{1,0:T(8,128)} %reshape.316, f32[256]{0:T(256)S(1)} %get-tuple-element.105), kind=kCustom, calls=%fused_computation.65 | custom fusion | flops 524288 | bytes 4195328 | tf_op jit(solution)/shard_map/scatter-add | solution.py:83
  139.9 7.0 %scatter_custom_fusion.3 = f32[768,1024]{1,0:T(8,128)} fusion(f32[768,1024]{1,0:T(8,128)} %scatter_custom_fusion.2, s32[256]{0:T(256)} %bitcast.270, f32[256,1024]{1,0:T(8,128)} %reshape.317, f32[256]{0:T(256)S(1)} %get-tuple-element.107), kind=kCustom, calls=%fused_computation.63 | custom fusion | flops 524288 | bytes 4195328 | tf_op jit(solution)/shard_map/scatter-add | solution.py:83
  146.9 7.0 %scatter_custom_fusion.4 = f32[768,1024]{1,0:T(8,128)} fusion(f32[768,1024]{1,0:T(8,128)} %scatter_custom_fusion.3, s32[256]{0:T(256)} %bitcast.271, f32[256,1024]{1,0:T(8,128)} %reshape.318, f32[256]{0:T(256)S(1)} %get-tuple-element.109), kind=kCustom, calls=%fused_computation.61 | custom fusion | flops 524288 | bytes 4195328 | tf_op jit(solution)/shard_map/scatter-add | solution.py:83
  153.9 6.5 %scatter_custom_fusion.5 = f32[768,1024]{1,0:T(8,128)} fusion(f32[768,1024]{1,0:T(8,128)} %scatter_custom_fusion.4, s32[256]{0:T(256)} %bitcast.272, f32[256,1024]{1,0:T(8,128)S(1)} %reshape.319, f32[256]{0:T(256)S(1)} %get-tuple-element.111), kind=kCustom, calls=%fused_computation.59 | custom fusion | flops 524288 | bytes 4195328 | tf_op jit(solution)/shard_map/scatter-add | solution.py:83
  160.3 6.5 %scatter_custom_fusion.6 = f32[768,1024]{1,0:T(8,128)} fusion(f32[768,1024]{1,0:T(8,128)} %scatter_custom_fusion.5, s32[256]{0:T(256)} %bitcast.273, f32[256,1024]{1,0:T(8,128)S(1)} %reshape.320, f32[256]{0:T(256)S(1)} %get-tuple-element.45), kind=kCustom, calls=%fused_computation.57 | custom fusion | flops 524288 | bytes 4195328 | tf_op jit(solution)/shard_map/scatter-add | solution.py:83
  166.8 2.2 convert.4
  170.0 4.6 %collective-permute-start.3 = (bf16[256,1024]{1,0:T(8,128)(2,1)}, bf16[256,1024]{1,0:T(8,128)(2,1)}, u32[]{:S(2)}, u32[]{:S(2)}) collective-permute-start(bf16[256,1024]{1,0:T(8,128)(2,1)} %get-tuple-element.86), channel_id=1, source_target_pairs={{0,15},{1,0},{2,1},{3,2},{4,3},{5,4},{6,5},{7,6},{8,7},{9,8},{10,9... | collective-permute-start | bytes 1572872 | tf_op jit(solution)/shard_map/ppermute | solution.py:25
  175.1 2.7 fusion.119
  177.9 2.7 convolution_bitcast_fusion
  182.4 59.1 %psum.15 = f32[7,16,16]{2,1,0:T(8,128)S(1)} all-reduce(f32[7,16,16]{2,1,0:T(8,128)S(1)} %constant_dynamic-update-slice_fusion.3), channel_id=1, replica_groups=mesh['group'=2,'space'=16] {'space'}, use_global_device_ids=true, to_apply=%region_15.18 | all-reduce | flops 1792 | bytes 14336 | tf_op jit(solution)/shard_map/psum | solution.py:89
  242.1 2.6 fusion.11
  244.7 42.8 %all-reduce.2.cloned.1.call-done = f32[1024,1024]{1,0:T(8,128)} async-done(((f32[1024,1024]{1,0:T(8,128)}), f32[1024,1024]{1,0:T(8,128)}) %all-reduce.2.cloned.1.call-update) | async-done | bytes 4194320 | tf_op jit(solution)/shard_map/psum | solution.py:89
  (176 shorter events, 76.0 us)
Async XLA Ops:
  7.2 25.4 %copy-start = (bf16[1024,1024]{1,0:T(8,128)(2,1)S(1)}, bf16[1024,1024]{1,0:T(8,128)(2,1)}, u32[]{:S(2)}) copy-start(bf16[1024,1024]{1,0:T(8,128)(2,1)} %param.22) | copy-start | bytes 6291460
  7.2 13.1 %copy-start.2 = (s32[256,7]{0,1:T(8,128)S(1)}, s32[256,7]{0,1:T(8,128)}, u32[]{:S(2)}) copy-start(s32[256,7]{0,1:T(8,128)} %param.23) | copy-start | bytes 21508
  7.2 280.3 %all-reduce.2.cloned.1.call-start = ((), (), s32[]{:S(2)}) async-start(), calls=%async_computation | async-start | bytes 8388608 | tf_op jit(solution)/shard_map/psum | solution.py:89
  7.2 30.1 %collective-permute-start = (bf16[256,1024]{1,0:T(8,128)(2,1)}, bf16[256,1024]{1,0:T(8,128)(2,1)}, u32[]{:S(2)}, u32[]{:S(2)}) collective-permute-start(bf16[256,1024]{1,0:T(8,128)(2,1)} %param.19), channel_id=1, source_target_pairs={{0,1},{1,2},{2,3},{3,4},{4,5},{5,6},{6,7},{7,8},{8,9},{9,10},{10,1... | collective-permute-start | bytes 1572872 | tf_op jit(solution)/shard_map/ppermute | solution.py:15
  7.7 31.8 %collective-permute-start.1 = (bf16[256,1024]{1,0:T(8,128)(2,1)}, bf16[256,1024]{1,0:T(8,128)(2,1)}, u32[]{:S(2)}, u32[]{:S(2)}) collective-permute-start(bf16[256,1024]{1,0:T(8,128)(2,1)} %param.19), channel_id=1, source_target_pairs={{1,0},{2,1},{3,2},{4,3},{5,4},{6,5},{7,6},{8,7},{9,8},{10,9},{11,1... | collective-permute-start | bytes 1572872 | tf_op jit(solution)/shard_map/ppermute | solution.py:18
  19.6 12.9 %copy-start.3 = (bf16[256,1024]{1,0:T(8,128)(2,1)S(1)}, bf16[256,1024]{1,0:T(8,128)(2,1)}, u32[]{:S(2)}) copy-start(bf16[256,1024]{1,0:T(8,128)(2,1)} %param.20) | copy-start | bytes 1572868
  34.3 1.6 copy-start.12
  34.5 2.8 copy-start.21
  49.7 22.9 %copy-start.4 = (bf16[2048,128]{1,0:T(8,128)(2,1)}, bf16[2048,128]{1,0:T(8,128)(2,1)S(1)}, u32[]{:S(2)}) copy-start(bf16[2048,128]{1,0:T(8,128)(2,1)S(1)} %reshape.309) | copy-start | bytes 1572868
  69.7 2.6 copy-start.10
  71.9 1.1 copy-start.6
  72.6 1.1 copy-start.7
  73.0 1.1 copy-start.8
  73.7 1.1 copy-start.16
  73.7 1.4 copy-start.18
  82.4 5.0 %copy-start.11 = (bf16[2048,128]{1,0:T(8,128)(2,1)S(1)}, bf16[2048,128]{1,0:T(8,128)(2,1)}, u32[]{:S(2)}) copy-start(bf16[2048,128]{1,0:T(8,128)(2,1)} %reshape.307) | copy-start | bytes 1572868
  88.4 2.8 copy-start.20
  88.4 7.6 %copy-start.5 = (bf16[2048,128]{1,0:T(8,128)(2,1)S(1)}, bf16[2048,128]{1,0:T(8,128)(2,1)}, u32[]{:S(2)}) copy-start(bf16[2048,128]{1,0:T(8,128)(2,1)} %copy-done.4) | copy-start | bytes 1572868
  100.6 2.2 copy-start.9
  102.2 5.9 %copy-start.17 = (bf16[2048,128]{1,0:T(8,128)(2,1)S(1)}, bf16[2048,128]{1,0:T(8,128)(2,1)}, u32[]{:S(2)}) copy-start(bf16[2048,128]{1,0:T(8,128)(2,1)} %reshape.313) | copy-start | bytes 1572868
  102.8 6.3 %copy-start.13 = (f32[2048,128]{1,0:T(8,128)S(1)}, f32[2048,128]{1,0:T(8,128)}, u32[]{:S(2)}) copy-start(f32[2048,128]{1,0:T(8,128)} %fusion.112) | copy-start | bytes 3145732
  110.3 4.9 %copy-start.14 = (f32[2048,128]{1,0:T(8,128)S(1)}, f32[2048,128]{1,0:T(8,128)}, u32[]{:S(2)}) copy-start(f32[2048,128]{1,0:T(8,128)} %fusion.115) | copy-start | bytes 3145732
  110.3 6.1 %copy-start.15 = (f32[2048,128]{1,0:T(8,128)S(1)}, f32[2048,128]{1,0:T(8,128)}, u32[]{:S(2)}) copy-start(f32[2048,128]{1,0:T(8,128)} %fusion.116) | copy-start | bytes 3145732
  166.8 7.8 %copy-start.19 = (bf16[2048,128]{0,1:T(8,128)(2,1)S(1)}, bf16[2048,128]{0,1:T(8,128)(2,1)}, u32[]{:S(2)}) copy-start(bf16[2048,128]{0,1:T(8,128)(2,1)} %get-tuple-element.87) | copy-start | bytes 1572868
  170.0 72.1 %collective-permute-start.2 = (bf16[256,1024]{1,0:T(8,128)(2,1)}, bf16[256,1024]{1,0:T(8,128)(2,1)}, u32[]{:S(2)}, u32[]{:S(2)}) collective-permute-start(bf16[256,1024]{1,0:T(8,128)(2,1)} %get-tuple-element.85), channel_id=1, source_target_pairs={{0,1},{1,2},{2,3},{3,4},{4,5},{5,6},{6,7},{7,8},{8,9},{9,10},{10,1... | collective-permute-start | bytes 1572872 | tf_op jit(solution)/shard_map/ppermute | solution.py:25
  170.0 72.1 %collective-permute-start.3 = (bf16[256,1024]{1,0:T(8,128)(2,1)}, bf16[256,1024]{1,0:T(8,128)(2,1)}, u32[]{:S(2)}, u32[]{:S(2)}) collective-permute-start(bf16[256,1024]{1,0:T(8,128)(2,1)} %get-tuple-element.86), channel_id=1, source_target_pairs={{0,15},{1,0},{2,1},{3,2},{4,3},{5,4},{6,5},{7,6},{8,7},{9,8},{10,9... | collective-permute-start | bytes 1572872 | tf_op jit(solution)/shard_map/ppermute | solution.py:25
  177.9 111.3 %copy-start.1 = (bf16[1024,1024]{1,0:T(8,128)(2,1)S(1)}, bf16[1024,1024]{1,0:T(8,128)(2,1)}, u32[]{:S(2)}) copy-start(bf16[1024,1024]{1,0:T(8,128)(2,1)} %param.22) | copy-start | bytes 6291460
Sparse Core Ops, SparseCore 0:
  178.0 109.4 all-reduce.1
where the time goes:
time: 302 us; the launch traced here: 296 us
  local copies, waits for them, and re-layouts  70.5 us (23%)
  other arithmetic  68 us (23%)
  blocking collectives  59.1 us (20%)
  waiting for transfers between devices  42.8 us (14%)
  matrix products  30.7 us (10%)
  between operations  14.9 us (5%)
  starting transfers between devices  10.2 us (3%)
    psum x1, blocking collectives, shards(): mix_total, conv_total = lax.psum((local_mix, local_conv), 'space')  59.1 us
    scatter-add x7, other arithmetic, shards(): spread = spread.at[local_index].add(tap_term)  46.5 us
    psum x1, waiting for transfers between devices, shards(): mix_total, conv_total = lax.psum((local_mix, local_conv), 'space')  42.8 us
    gather x7, local copies, waits for them, and re-layouts, shards(): source = jnp.take_along_axis(neighbours, slot_index[:, None], axis=1)[:, 0]  13.8 us
    dot_general x7, matrix products, shards(): lax.dot_general(tap_rows, grad_pre, (((0,), (0,)), ((), ())), preferred_e...  13 us
    gather x7, local copies, waits for them, and re-layouts, shards(): jnp.take(extended, local_index, axis=0)  11.3 us
    reshape x7, local copies, waits for them, and re-layouts, shards(): tap_term = lax.dot_general(grad_pre, wide_weights[index_tap], (((1,), (1,...  11.1 us
    reshape x7, local copies, waits for them, and re-layouts, shards(): tap_rows = tap_rows.reshape(flat_rows, lane_width)  10.8 us
  transfers between devices with their start and end apart: 5, of which 1 were waited for; matrix products, arithmetic and copies ran while one was open for 13% of the time, Pallas kernels for 0%

commit v1 on v0

v1 whole, which is shorter than its diff:
```python
import functools

import jax
import jax.numpy as jnp
from jax import lax
from jax.experimental import pallas as pl
from jax.experimental.pallas import tpu as pltpu
from jax.sharding import PartitionSpec as P

ROW = 256
LANES = 256
F32 = jnp.float32
BF16 = jnp.bfloat16


def dot(a, b, dims=((1,), (0,)), precision=None):
    return lax.dot_general(a, b, (dims, ((), ())), preferred_element_type=F32, precision=precision)


def remote(src, dst, send, recv, target):
    return pltpu.make_async_remote_copy(
        src_ref=src,
        dst_ref=dst,
        send_sem=send,
        recv_sem=recv,
        device_id={"space": target},
        device_id_type=pl.DeviceIdType.MESH,
    )


def kernel(
    devices,
    x_ref, cot_ref, conv_ref, mix_ref, idx_ref, idx_t_ref,
    grad_ref, gmix_ref, gconv_ref,
    ext, hot, hot_t, wide, wide_t, ups, taps, gpre, terms, spread_mid, edges, edges_in,
    part, part_in, summed, summed_in, conv_acc, conv_own, conv_in,
    halo_send, halo_recv, edge_send, edge_recv, core_send, core_recv, chip_send, chip_recv,
    conv_send, conv_recv,
):
    tile, features = x_ref.shape
    taps_n, channels, _ = conv_ref.shape
    blocks = features // LANES
    share = features // devices
    chips = devices // 2
    owners = LANES // share
    me = lax.axis_index("space")
    nxt, prv = lax.rem(me + 1, devices), lax.rem(me + devices - 1, devices)
    core = lax.rem(me, 2)
    chip = me // 2
    twin = chip * 2 + (1 - core)

    barrier = pltpu.get_barrier_semaphore()

    @pl.loop(1, devices)
    def _(d):
        pl.semaphore_signal(
            barrier, inc=1, device_id={"space": lax.rem(me + d, devices)},
            device_id_type=pl.DeviceIdType.MESH,
        )

    pl.semaphore_wait(barrier, devices - 1)

    to_next = remote(x_ref, ext.at[pl.ds(0, ROW)], halo_send.at[0], halo_recv.at[0], nxt)
    to_prev = remote(x_ref, ext.at[pl.ds(ROW + tile, ROW)], halo_send.at[1], halo_recv.at[1], prv)
    to_next.start()
    to_prev.start()

    ext[ROW : ROW + tile, :] = x_ref[...]
    width = tile + 2 * ROW
    lane_ids = lax.broadcasted_iota(jnp.int32, (tile, width), 1)
    row_ids = lax.broadcasted_iota(jnp.int32, (width, tile), 0)
    for j in range(1, taps_n):
        hot[(j - 1) * tile : j * tile, :] = (lane_ids == idx_ref[:, j : j + 1]).astype(F32).astype(BF16)
        hot_t[:, (j - 1) * tile : j * tile] = (row_ids == idx_t_ref[j : j + 1, :]).astype(F32).astype(BF16)
    spot = lax.broadcasted_iota(jnp.int32, (LANES, channels), 0) % channels
    pick = (spot == lax.broadcasted_iota(jnp.int32, (LANES, channels), 1)).astype(F32).astype(BF16)
    same = (
        lax.broadcasted_iota(jnp.int32, (LANES, LANES), 0) // channels
        == lax.broadcasted_iota(jnp.int32, (LANES, LANES), 1) // channels
    )
    for j in range(taps_n):
        w = conv_ref[j]
        full = dot(dot(pick, w).astype(BF16), pick, ((1,), (1,)))
        wide[j * LANES : (j + 1) * LANES, :] = jnp.where(same, full, 0.0).astype(BF16)
        full_t = dot(dot(pick, w, ((1,), (1,))).astype(BF16), pick, ((1,), (1,)))
        wide_t[:, j * LANES : (j + 1) * LANES] = jnp.where(same, full_t, 0.0).astype(BF16)

    @pl.loop(0, blocks)
    def _(k):
        rows = pl.ds(pl.multiple_of(k * LANES, LANES), LANES)
        ups[k] = dot(cot_ref[...], mix_ref[rows, :], ((1,), (1,)))

    to_next.wait()
    to_prev.wait()

    def core_copy(k):
        per = owners // 2
        at = pl.ds(k * per, per)
        return remote(
            part.at[1 - core, at], part_in.at[at], core_send.at[k], core_recv.at[k], twin
        )

    @pl.loop(0, blocks)
    def _(k):
        cols = pl.ds(pl.multiple_of(k * LANES, LANES), LANES)
        source = ext[:, cols]
        taps[k, :, 0:LANES] = ext[ROW : ROW + tile, cols]
        for j in range(1, taps_n):
            taps[k, :, j * LANES : (j + 1) * LANES] = dot(
                hot[(j - 1) * tile : j * tile, :], source
            ).astype(BF16)
        pre = dot(taps[k], wide[...])
        square = pre * pre
        scale = 0.7978845608028654
        t = jnp.tanh(scale * pre * (1.0 + 0.044715 * square))
        half = 0.5 * (1.0 + t)
        active = (pre * half).astype(BF16)
        slope = half + 0.5 * pre * (1.0 - t * t) * scale * (1.0 + 3 * 0.044715 * square)
        gpre[k] = (ups[k] * slope).astype(BF16)
        local = dot(active, cot_ref[...], ((0,), (0,))).astype(BF16)
        for i in range(owners):
            part[i % 2, k * (owners // 2) + i // 2] = local[i * share : (i + 1) * share, :]
        core_copy(k).start()

    def chip_copy(d):
        target = lax.rem(chip + d, chips)
        return remote(
            summed.at[target], summed_in.at[d], chip_send.at[d], chip_recv.at[d],
            target * 2 + core,
        )

    @pl.loop(0, blocks)
    def _(k):
        core_copy(k).wait()

    @pl.loop(0, chips)
    def _(h):
        summed[h] = (part[core, h].astype(F32) + part_in[h].astype(F32)).astype(BF16)

    @pl.loop(1, chips)
    def _(d):
        chip_copy(d).start()

    @pl.loop(0, blocks)
    def _(k):
        cols = pl.ds(pl.multiple_of(k * LANES, LANES), LANES)
        g = gpre[k]
        own = dot(g, wide_t[:, 0:LANES]) + cot_ref[:, cols].astype(F32)
        for j in range(1, taps_n):
            terms[(j - 1) * tile : j * tile, :] = dot(
                g, wide_t[:, j * LANES : (j + 1) * LANES]
            ).astype(BF16)
        edges[0, :, cols] = dot(hot_t[0:ROW, :], terms[...]).astype(BF16)
        spread_mid[:, cols] = own + dot(hot_t[ROW : ROW + tile, :], terms[...])
        edges[1, :, cols] = dot(hot_t[ROW + tile :, :], terms[...]).astype(BF16)

    edge_prev = remote(edges.at[0], edges_in.at[0], edge_send.at[0], edge_recv.at[0], prv)
    edge_next = remote(edges.at[1], edges_in.at[1], edge_send.at[1], edge_recv.at[1], nxt)
    edge_prev.start()
    edge_next.start()

    conv_acc[...] = jnp.zeros_like(conv_acc)

    @pl.loop(0, blocks)
    def _(k):
        conv_acc[...] += dot(gpre[k], taps[k], ((0,), (0,)))

    rows_same = lax.broadcasted_iota(jnp.int32, (LANES, LANES), 0) // channels
    cols_same = lax.broadcasted_iota(jnp.int32, (LANES, LANES), 1) // channels
    out_lane = lax.broadcasted_iota(jnp.int32, (LANES, 128), 1)
    in_place = lax.broadcasted_iota(jnp.int32, (LANES, 128), 0) % channels
    total = jnp.zeros((channels, 128), F32)
    for j in range(taps_n):
        block = jnp.where(rows_same == cols_same, conv_acc[:, j * LANES : (j + 1) * LANES], 0.0)
        folded = block[0:channels, :]
        for l in range(1, LANES // channels):
            folded = folded + block[l * channels : (l + 1) * channels, :]
        place = (out_lane == in_place + j * channels).astype(F32)
        total = total + dot(folded, place, precision=lax.Precision.HIGHEST)
    conv_own[...] = total

    def conv_copy(d):
        return remote(
            conv_own, conv_in.at[d], conv_send.at[d], conv_recv.at[d], lax.rem(me + d, devices)
        )

    @pl.loop(1, devices)
    def _(d):
        conv_copy(d).start()

    edge_prev.wait()
    edge_next.wait()
    first, last = edges_in[1].astype(F32), edges_in[0].astype(F32)
    if tile == ROW:
        grad_ref[...] = (spread_mid[...] + first + last).astype(BF16)
    else:
        spread_mid[0:ROW, :] += first
        spread_mid[tile - ROW :, :] += last
        grad_ref[...] = spread_mid[...].astype(BF16)

    conv_in[0] = conv_own[...]

    @pl.loop(1, devices)
    def _(d):
        conv_copy(d).wait()

    def add_conv(owner, acc):
        return acc + conv_in[lax.rem(me - owner + devices, devices)]

    gconv_ref[...] = lax.fori_loop(0, devices, add_conv, jnp.zeros((channels, 128), F32)) * (
        1.0 / (devices * tile * (features // channels)) ** 0.5
    )

    gmix_ref[...] = part[core, chip].astype(F32) + part_in[chip].astype(F32)

    @pl.loop(1, chips)
    def _(d):
        chip_copy(d).wait()
        gmix_ref[...] += summed_in[d].astype(F32)

    gmix_ref[...] = gmix_ref[...] * (1.0 / (devices * tile) ** 0.5)


def shards(columns_in, cotangent, conv_weight, mix_weight, neighbours, rotations, pentagons):
    tile, features = columns_in.shape
    taps_n, channels, _ = conv_weight.shape
    devices = lax.axis_size("space")
    total_cols = tile * devices
    offset = lax.axis_index("space") * tile
    share = features // devices
    chips = devices // 2
    blocks = features // LANES
    width = tile + 2 * ROW

    taps_at = lax.broadcasted_iota(jnp.int32, (8, tile), 0)
    slot = jnp.where(taps_at == 0, 0, 1 + (taps_at - 1 - rotations[None, :]) % 6)
    near = (neighbours.T - offset + ROW) % total_cols
    source = jnp.zeros((8, tile), jnp.int32)
    for s in range(taps_n):
        source = jnp.where(slot == s, near[s : s + 1, :], source)
    index_t = jnp.where((slot == 6) & (pentagons[None, :] != 0), -1, source)
    index = index_t.T

    vmem = pl.BlockSpec(memory_space=pltpu.VMEM)
    grad_input, grad_mix, conv = pl.pallas_call(
        functools.partial(kernel, devices),
        out_shape=(
            jax.ShapeDtypeStruct((tile, features), BF16),
            jax.ShapeDtypeStruct((share, features), F32),
            jax.ShapeDtypeStruct((channels, 128), F32),
        ),
        in_specs=[vmem] * 6,
        out_specs=(vmem,) * 3,
        scratch_shapes=[
            pltpu.VMEM((width, features), BF16),
            pltpu.VMEM(((taps_n - 1) * tile, width), BF16),
            pltpu.VMEM((width, (taps_n - 1) * tile), BF16),
            pltpu.VMEM((taps_n * LANES, LANES), BF16),
            pltpu.VMEM((LANES, taps_n * LANES), BF16),
            pltpu.VMEM((blocks, tile, LANES), F32),
            pltpu.VMEM((blocks, tile, taps_n * LANES), BF16),
            pltpu.VMEM((blocks, tile, LANES), BF16),
            pltpu.VMEM(((taps_n - 1) * tile, LANES), BF16),
            pltpu.VMEM((tile, features), F32),
            pltpu.VMEM((2, ROW, features), BF16),
            pltpu.VMEM((2, ROW, features), BF16),
            pltpu.VMEM((2, chips, share, features), BF16),
            pltpu.VMEM((chips, share, features), BF16),
            pltpu.VMEM((chips, share, features), BF16),
            pltpu.VMEM((chips, share, features), BF16),
            pltpu.VMEM((LANES, taps_n * LANES), F32),
            pltpu.VMEM((channels, 128), F32),
            pltpu.VMEM((devices, channels, 128), F32),
            pltpu.SemaphoreType.DMA((2,)),
            pltpu.SemaphoreType.DMA((2,)),
            pltpu.SemaphoreType.DMA((2,)),
            pltpu.SemaphoreType.DMA((2,)),
            pltpu.SemaphoreType.DMA((blocks,)),
            pltpu.SemaphoreType.DMA((blocks,)),
            pltpu.SemaphoreType.DMA((chips,)),
            pltpu.SemaphoreType.DMA((chips,)),
            pltpu.SemaphoreType.DMA((devices,)),
            pltpu.SemaphoreType.DMA((devices,)),
        ],
        compiler_params=pltpu.CompilerParams(
            collective_id=0, has_side_effects=True, vmem_limit_bytes=52 * 1024 * 1024
        ),
    )(columns_in, cotangent, conv_weight, mix_weight, index, index_t)
    grad_conv = conv.reshape(channels, 128 // channels, channels)[:, :taps_n].transpose(1, 2, 0)
    return grad_input, grad_mix, grad_conv


def solution(mesh):
    return jax.shard_map(
        shards,
        mesh=mesh,
        in_specs=(
            P(("group", "space"), None),
            P(("group", "space"), None),
            P(),
            P(),
            P("space", None),
            P("space"),
            P("space"),
        ),
        out_specs=(P(("group", "space"), None), P("space", "group"), P("group", None, None)),
        check_vma=False,
    )
```

time: 302 us -> 71.9 us (0.24); the launches traced: 296 us -> 71.5 us
  local copies, waits for them, and re-layouts: 70.5 us -> 5.06 us
  other arithmetic: 68 us -> 3.23 us
  Pallas kernels: 0 us -> 62.6 us
  blocking collectives: 59.1 us -> 0 us
  waiting for transfers between devices: 42.8 us -> 0 us
  matrix products: 30.7 us -> 0 us
  between operations: 14.9 us -> 0.67 us
  starting transfers between devices: 10.2 us -> 0 us
    pallas_call x0 -> x1, Pallas kernels: none -> 62.6 us  [shards(): pl.pallas_call(functools.partial(kernel, devices), out_shape=(jax.ShapeDt...]
    psum x1 -> x0, blocking collectives: 59.1 us -> none  [shards(): mix_total, conv_total = lax.psum((local_mix, local_conv), 'space')]
    scatter-add x7 -> x0, other arithmetic: 46.5 us -> none  [shards(): spread = spread.at[local_index].add(tap_term)]
    psum x1 -> x0, waiting for transfers between devices: 42.8 us -> none  [shards(): mix_total, conv_total = lax.psum((local_mix, local_conv), 'space')]
    gather x21 -> x0, local copies, waits for them, and re-layouts: 34.4 us -> none  [the longest x7 13.8 us: shards(): source = jnp.take_along_axis(neighbours, slot_index[:, None], axis=1)[:, 0]]
    dot_general x23 -> x0, matrix products: 30.7 us -> none  [the longest x7 13 us: shards(): lax.dot_general(tap_rows, grad_pre, (((0,), (0,)), ((), ())), preferred_e...]
    reshape x17 -> x1, local copies, waits for them, and re-layouts: 23.4 us -> 0.1 us  [shards(): conv.reshape(channels, 128 // channels, channels)[:, :taps_n]]
    ppermute x4 -> x0, starting transfers between devices: 10.2 us -> none  [the longest x1 5.06 us: with_halo(): lax.ppermute(lax.slice_in_dim(block, 0, width, axis=dim), axis, backward)]
  transfers between devices with their start and end apart: 5 -> 0, of which waited for: 1 -> 0; matrix products, arithmetic and copies ran while one was open for 13% -> 0% of each run, Pallas kernels for 0% -> 0%
where the time goes in v1:
time: 71.9 us; the launch traced here: 71.5 us
  Pallas kernels  62.6 us (87%)
  local copies, waits for them, and re-layouts  5.06 us (7%)
  other arithmetic  3.23 us (4%)
    pallas_call x1, Pallas kernels, shards(): pl.pallas_call(functools.partial(kernel, devices), out_shape=(jax.ShapeDt...  62.6 us
    unnamed x8, local copies, waits for them, and re-layouts  4.32 us
    select_n x2, other arithmetic, shards(): index_t = jnp.where((slot == 6) & (pentagons[None, :] != 0), -1, source)  1.82 us

profile of v1, /device:TPU:0, one launch (start us, length us, event | category | flops | bytes accessed | tf_op | source)
XLA Modules:
  0.0 71.5 jit_solution(6132669599620119169)
XLA Ops:
  0.6 0.7 broadcast_compare_fusion
  1.3 0.7 add_select_fusion.2
  2.0 0.8 %select_select_fusion.1.idx_t_ref = s32[8,256]{1,0:T(8,128)S(1)} fusion(s32[256]{0:T(256)S(1)} %bitcast.17, s32[256]{0:T(256)S(1)} %bitcast.19, s32[256]{0:T(256)S(1)} %bitcast.21, s32[256]{0:T(256)S(1)} %bitcast.23, s32[256]{0:T(256)S(1)} %bitcast.25, s32[256]{0:T(256)S(1)} %bitcast.27, s32[256]{0:T(256)S(1)} %bitcast.15, s32[256]{0:T(256)} %param.12, ...), kind=kLoop, calls=%fused_computation.23 | loop fusion | flops 51200 | bytes 16680 | tf_op jit(solution)/shard_map/jit(_where)/select_n | solution.py:241
  2.8 1.1 %select_select_fusion.idx_ref = s32[256,8]{1,0:T(8,128)S(1)} fusion(s32[256]{0:T(256)S(1)} %bitcast.18, s32[256]{0:T(256)S(1)} %bitcast.20, s32[256]{0:T(256)S(1)} %bitcast.22, s32[256]{0:T(256)S(1)} %bitcast.24, s32[256]{0:T(256)S(1)} %bitcast.26, s32[256]{0:T(256)S(1)} %bitcast.28, s32[256]{0:T(256)S(1)} %bitcast.16, s32[256]{0:T(256)} %param.12, ...), kind=kLoop, calls=%fused_computation.3 | loop fusion | flops 51200 | bytes 16680 | tf_op jit(solution)/shard_map/jit(_where)/select_n | solution.py:241
  3.9 0.0 copy-start
  3.9 1.0 %copy-done = bf16[256,1024]{1,0:T(8,128)(2,1)S(1)} copy-done((bf16[256,1024]{1,0:T(8,128)(2,1)S(1)}, bf16[256,1024]{1,0:T(8,128)(2,1)}, u32[]{:S(2)}) %copy-start) | copy-done | bytes 524312
  4.9 0.0 copy-start.1
  4.9 1.0 %copy-done.1 = bf16[256,1024]{1,0:T(8,128)(2,1)S(1)} copy-done((bf16[256,1024]{1,0:T(8,128)(2,1)S(1)}, bf16[256,1024]{1,0:T(8,128)(2,1)}, u32[]{:S(2)}) %copy-start.1) | copy-done | bytes 524312
  6.0 0.0 copy-start.2
  6.0 0.7 %copy-done.2 = bf16[7,16,16]{2,1,0:T(8,128)(2,1)S(1)} copy-done((bf16[7,16,16]{2,1,0:T(8,128)(2,1)S(1)}, bf16[7,16,16]{2,1,0:T(8,128)(2,1)}, u32[]{:S(2)}) %copy-start.2) | copy-done | bytes 3608
  6.7 62.6 %shard_map.94 = (bf16[256,1024]{1,0:T(8,128)(2,1)S(1)}, f32[64,1024]{1,0:T(8,128)S(1)}, f32[16,128]{1,0:T(8,128)S(1)}) custom-call(bf16[256,1024]{1,0:T(8,128)(2,1)S(1)} %copy-done, bf16[256,1024]{1,0:T(8,128)(2,1)S(1)} %copy-done.1, bf16[7,16,16]{2,1,0:T(8,128)(2,1)S(1)} %copy-done.2, bf16[1024,1024]{1,0:T(8,128)(2,1)} %mix_ref.1, ...), custom_call_target="tpu_custom_call" | custom-call | tf_op jit(solution)/shard_map/pallas_call | solution.py:245
  69.3 0.1 copy.11
  69.4 0.6 slice_bitcast_fusion
  70.0 0.8 %copy.14 = bf16[256,1024]{1,0:T(8,128)(2,1)} copy(bf16[256,1024]{1,0:T(8,128)(2,1)S(1)} %get-tuple-element.19) | data formatting | bytes 1048576
  70.8 0.7 copy.15
  (3 shorter events, 0.0 us)
Async XLA Ops:
  3.9 1.0 %copy-start = (bf16[256,1024]{1,0:T(8,128)(2,1)S(1)}, bf16[256,1024]{1,0:T(8,128)(2,1)}, u32[]{:S(2)}) copy-start(bf16[256,1024]{1,0:T(8,128)(2,1)} %x_ref.1) | copy-start | bytes 1572868
  4.9 1.0 %copy-start.1 = (bf16[256,1024]{1,0:T(8,128)(2,1)S(1)}, bf16[256,1024]{1,0:T(8,128)(2,1)}, u32[]{:S(2)}) copy-start(bf16[256,1024]{1,0:T(8,128)(2,1)} %cot_ref.1) | copy-start | bytes 1572868
  6.0 0.7 %copy-start.2 = (bf16[7,16,16]{2,1,0:T(8,128)(2,1)S(1)}, bf16[7,16,16]{2,1,0:T(8,128)(2,1)}, u32[]{:S(2)}) copy-start(bf16[7,16,16]{2,1,0:T(8,128)(2,1)} %conv_ref.1) | copy-start | bytes 10756

commit v2 on v1

v2 whole, which is shorter than its diff:
```python
import functools

import jax
import jax.numpy as jnp
from jax import lax
from jax.experimental import pallas as pl
from jax.experimental.pallas import tpu as pltpu
from jax.sharding import PartitionSpec as P

ROW = 256
LANES = 256
F32 = jnp.float32
BF16 = jnp.bfloat16


def dot(a, b, dims=((1,), (0,)), precision=None):
    return lax.dot_general(a, b, (dims, ((), ())), preferred_element_type=F32, precision=precision)


def remote(src, dst, send, recv, target):
    return pltpu.make_async_remote_copy(
        src_ref=src,
        dst_ref=dst,
        send_sem=send,
        recv_sem=recv,
        device_id={"space": target},
        device_id_type=pl.DeviceIdType.MESH,
    )


def kernel(
    devices,
    x_ref, cot_hbm, conv_hbm, mix_hbm, near_hbm, rot_hbm, pent_hbm,
    grad_ref, gmix_ref, gconv_ref,
    cot_ref, conv_ref, mix_ref, near_ref, rot_ref, pent_ref, index_pad,
    ext, hot, hot_t, wide, wide_t, ups, taps, gpre, terms, spread_mid, edges, edges_in,
    part, part_in, summed, summed_in, conv_acc, conv_own, conv_in,
    load_sem, mid_sem, halo_send, halo_recv, edge_send, edge_recv, core_send, core_recv,
    chip_send, chip_recv, conv_send, conv_recv,
):
    tile, features = x_ref.shape
    taps_n, channels, _ = conv_ref.shape
    blocks = features // LANES
    share = features // devices
    chips = devices // 2
    owners = LANES // share
    total_cols = tile * devices
    width = tile + 2 * ROW
    me = lax.axis_index("space")
    nxt, prv = lax.rem(me + 1, devices), lax.rem(me + devices - 1, devices)
    core = lax.rem(me, 2)
    chip = me // 2
    twin = chip * 2 + (1 - core)

    barrier = pltpu.get_barrier_semaphore()

    @pl.loop(1, devices)
    def _(d):
        pl.semaphore_signal(
            barrier, inc=1, device_id={"space": lax.rem(me + d, devices)},
            device_id_type=pl.DeviceIdType.MESH,
        )

    loads = [
        pltpu.make_async_copy(source, target, load_sem.at[n])
        for n, (source, target) in enumerate([
            (near_hbm, near_ref), (rot_hbm, rot_ref), (pent_hbm, pent_ref),
            (conv_hbm, conv_ref), (cot_hbm, cot_ref), (mix_hbm, mix_ref),
        ])
    ]
    for load in loads:
        load.start()

    def lanes(k):
        return pl.ds(pl.multiple_of(k * LANES, LANES), LANES)

    def block_at(i, device):
        return lax.rem(i + 1 + device // owners, blocks)

    def mid_copy(k):
        return pltpu.make_async_copy(
            x_ref.at[:, lanes(k)], ext.at[k, pl.ds(ROW, tile)], mid_sem.at[k]
        )

    def halo_next(k):
        return remote(
            x_ref.at[pl.ds(tile - ROW, ROW), lanes(k)], ext.at[k, pl.ds(0, ROW)],
            halo_send.at[0, k], halo_recv.at[0, k], nxt,
        )

    def halo_prev(k):
        return remote(
            x_ref.at[pl.ds(0, ROW), lanes(k)], ext.at[k, pl.ds(ROW + tile, ROW)],
            halo_send.at[1, k], halo_recv.at[1, k], prv,
        )

    def edge_prev(k):
        return remote(
            edges.at[0, k], edges_in.at[0, k], edge_send.at[0, k], edge_recv.at[0, k], prv
        )

    def edge_next(k):
        return remote(
            edges.at[1, k], edges_in.at[1, k], edge_send.at[1, k], edge_recv.at[1, k], nxt
        )

    @pl.loop(0, blocks)
    def _(i):
        mid_copy(block_at(i, me)).start()

    pl.semaphore_wait(barrier, devices - 1)

    @pl.loop(0, blocks)
    def _(i):
        halo_next(block_at(i, nxt)).start()
        halo_prev(block_at(i, prv)).start()

    for load in loads[:4]:
        load.wait()
    index_pad[...] = jnp.zeros_like(index_pad)
    away = near_ref[...] - me * tile
    away = jnp.where(away < 0, away + total_cols, away) + ROW
    away = jnp.where(away >= total_cols, away - total_cols, away)
    tap_ids = lax.broadcasted_iota(jnp.int32, (8, tile), 0)
    slot = tap_ids - 1 - jnp.broadcast_to(rot_ref[...], (8, tile))
    slot = jnp.where(tap_ids == 0, 0, 1 + jnp.where(slot < 0, slot + 6, slot))
    found = jnp.zeros((8, tile), jnp.int32)
    for n in range(taps_n):
        found = jnp.where(slot == n, jnp.broadcast_to(away[n : n + 1, :], (8, tile)), found)
    void = (slot == 6) & (jnp.broadcast_to(pent_ref[...], (8, tile)) != 0)
    found = jnp.where(void, -1, found)
    index_pad[0:8, :] = found
    index = index_pad[...].T

    spot = lax.broadcasted_iota(jnp.int32, (LANES, channels), 0) % channels
    pick = (spot == lax.broadcasted_iota(jnp.int32, (LANES, channels), 1)).astype(F32).astype(BF16)
    same = (
        lax.broadcasted_iota(jnp.int32, (LANES, LANES), 0) // channels
        == lax.broadcasted_iota(jnp.int32, (LANES, LANES), 1) // channels
    )
    for j in range(taps_n):
        w = conv_ref[j]
        full = dot(dot(pick, w).astype(BF16), pick, ((1,), (1,)))
        wide[j * LANES : (j + 1) * LANES, :] = jnp.where(same, full, 0.0).astype(BF16)
        full_t = dot(dot(pick, w, ((1,), (1,))).astype(BF16), pick, ((1,), (1,)))
        wide_t[:, j * LANES : (j + 1) * LANES] = jnp.where(same, full_t, 0.0).astype(BF16)
    lane_ids = lax.broadcasted_iota(jnp.int32, (tile, width), 1)
    row_ids = lax.broadcasted_iota(jnp.int32, (width, tile), 0)
    for j in range(1, taps_n):
        hot[(j - 1) * tile : j * tile, :] = (lane_ids == index[:, j : j + 1]).astype(F32).astype(BF16)
        hot_t[:, (j - 1) * tile : j * tile] = (row_ids == found[j : j + 1, :]).astype(F32).astype(BF16)

    for load in loads[4:]:
        load.wait()

    @pl.loop(0, blocks)
    def _(k):
        ups[k] = dot(cot_ref[...], mix_ref[lanes(k), :], ((1,), (1,)))

    conv_acc[...] = jnp.zeros_like(conv_acc)

    def core_copy(k):
        per = owners // 2
        at = pl.ds(k * per, per)
        return remote(
            part.at[1 - core, at], part_in.at[at], core_send.at[k], core_recv.at[k], twin
        )

    def chip_copy(target, d):
        return remote(
            summed.at[target], summed_in.at[d], chip_send.at[d], chip_recv.at[d],
            target * 2 + core,
        )

    def pass_on(k):
        core_copy(k).wait()

        @pl.loop(0, owners // 2)
        def _(n):
            h = k * (owners // 2) + n
            summed[h] = (part[core, h].astype(F32) + part_in[h].astype(F32)).astype(BF16)

            @pl.when(h != chip)
            def _():
                chip_copy(h, lax.rem(h - chip + chips, chips)).start()

    @pl.loop(0, blocks)
    def _(i):
        k = block_at(i, me)
        cols = lanes(k)
        mid_copy(k).wait()
        halo_next(k).wait_recv()
        halo_prev(k).wait_recv()
        source = ext[k]
        taps[k, :, 0:LANES] = ext[k, ROW : ROW + tile, :]
        for j in range(1, taps_n):
            taps[k, :, j * LANES : (j + 1) * LANES] = dot(
                hot[(j - 1) * tile : j * tile, :], source
            ).astype(BF16)
        pre = dot(taps[k], wide[...])
        square = pre * pre
        scale = 0.7978845608028654
        t = jnp.tanh(scale * pre * (1.0 + 0.044715 * square))
        half = 0.5 * (1.0 + t)
        active = (pre * half).astype(BF16)
        slope = half + 0.5 * pre * (1.0 - t * t) * scale * (1.0 + 3 * 0.044715 * square)
        gpre[k] = (ups[k] * slope).astype(BF16)
        local = dot(active, cot_ref[...], ((0,), (0,))).astype(BF16)
        for n in range(owners):
            part[n % 2, k * (owners // 2) + n // 2] = local[n * share : (n + 1) * share, :]
        core_copy(k).start()

        g = gpre[k]
        for j in range(1, taps_n):
            terms[(j - 1) * tile : j * tile, :] = dot(
                g, wide_t[:, j * LANES : (j + 1) * LANES]
            ).astype(BF16)
        edges[0, k] = dot(hot_t[0:ROW, :], terms[...]).astype(BF16)
        edge_prev(k).start()
        edges[1, k] = dot(hot_t[ROW + tile :, :], terms[...]).astype(BF16)
        edge_next(k).start()
        pass_on(k)
        own = dot(g, wide_t[:, 0:LANES]) + cot_ref[:, cols].astype(F32)
        spread_mid[k] = own + dot(hot_t[ROW : ROW + tile, :], terms[...])
        conv_acc[...] += dot(g, taps[k], ((0,), (0,)))

    rows_same = lax.broadcasted_iota(jnp.int32, (LANES, LANES), 0) // channels
    cols_same = lax.broadcasted_iota(jnp.int32, (LANES, LANES), 1) // channels
    out_lane = lax.broadcasted_iota(jnp.int32, (LANES, 128), 1)
    in_place = lax.broadcasted_iota(jnp.int32, (LANES, 128), 0) % channels
    total = jnp.zeros((channels, 128), F32)
    for j in range(taps_n):
        block = jnp.where(rows_same == cols_same, conv_acc[:, j * LANES : (j + 1) * LANES], 0.0)
        folded = block[0:channels, :]
        for l in range(1, LANES // channels):
            folded = folded + block[l * channels : (l + 1) * channels, :]
        place = (out_lane == in_place + j * channels).astype(F32)
        total = total + dot(folded, place, precision=lax.Precision.HIGHEST)
    conv_own[...] = total

    def conv_copy(d):
        return remote(
            conv_own, conv_in.at[d], conv_send.at[d], conv_recv.at[d], lax.rem(me + d, devices)
        )

    @pl.loop(1, devices)
    def _(d):
        conv_copy(d).start()

    @pl.loop(0, blocks)
    def _(i):
        k = block_at(i, me)
        edge_prev(k).wait_recv()
        edge_next(k).wait_recv()
        spread_mid[k, 0:ROW, :] += edges_in[1, k].astype(F32)
        spread_mid[k, tile - ROW :, :] += edges_in[0, k].astype(F32)
        grad_ref[:, lanes(k)] = spread_mid[k].astype(BF16)

    conv_in[0] = conv_own[...]

    @pl.loop(1, devices)
    def _(d):
        conv_copy(d).wait()

    def add_conv(owner, acc):
        return acc + conv_in[lax.rem(me - owner + devices, devices)]

    gconv_ref[...] = lax.fori_loop(0, devices, add_conv, jnp.zeros((channels, 128), F32)) * (
        1.0 / (devices * tile * (features // channels)) ** 0.5
    )

    gmix_ref[...] = part[core, chip].astype(F32) + part_in[chip].astype(F32)

    @pl.loop(1, chips)
    def _(d):
        chip_copy(lax.rem(chip + d, chips), d).wait()
        gmix_ref[...] += summed_in[d].astype(F32)

    gmix_ref[...] = gmix_ref[...] * (1.0 / (devices * tile) ** 0.5)

    @pl.loop(0, blocks)
    def _(k):
        halo_next(k).wait_send()
        halo_prev(k).wait_send()
        edge_prev(k).wait_send()
        edge_next(k).wait_send()


def shards(columns_in, cotangent, conv_weight, mix_weight, neighbours, rotations, pentagons):
    tile, features = columns_in.shape
    taps_n, channels, _ = conv_weight.shape
    devices = lax.axis_size("space")
    share = features // devices
    chips = devices // 2
    blocks = features // LANES
    width = tile + 2 * ROW

    vmem = pl.BlockSpec(memory_space=pltpu.VMEM)
    grad_input, grad_mix, conv = pl.pallas_call(
        functools.partial(kernel, devices),
        out_shape=(
            jax.ShapeDtypeStruct((tile, features), BF16),
            jax.ShapeDtypeStruct((share, features), F32),
            jax.ShapeDtypeStruct((channels, 128), F32),
        ),
        in_specs=[pl.BlockSpec(memory_space=pltpu.HBM)] * 7,
        out_specs=(vmem,) * 3,
        scratch_shapes=[
            pltpu.VMEM((tile, features), BF16),
            pltpu.VMEM((taps_n, channels, channels), BF16),
            pltpu.VMEM((features, features), BF16),
            pltpu.VMEM((taps_n, tile), jnp.int32),
            pltpu.VMEM((1, tile), jnp.int32),
            pltpu.VMEM((1, tile), jnp.int32),
            pltpu.VMEM((128, tile), jnp.int32),
            pltpu.VMEM((blocks, width, LANES), BF16),
            pltpu.VMEM(((taps_n - 1) * tile, width), BF16),
            pltpu.VMEM((width, (taps_n - 1) * tile), BF16),
            pltpu.VMEM((taps_n * LANES, LANES), BF16),
            pltpu.VMEM((LANES, taps_n * LANES), BF16),
            pltpu.VMEM((blocks, tile, LANES), F32),
            pltpu.VMEM((blocks, tile, taps_n * LANES), BF16),
            pltpu.VMEM((blocks, tile, LANES), BF16),
            pltpu.VMEM(((taps_n - 1) * tile, LANES), BF16),
            pltpu.VMEM((blocks, tile, LANES), F32),
            pltpu.VMEM((2, blocks, ROW, LANES), BF16),
            pltpu.VMEM((2, blocks, ROW, LANES), BF16),
            pltpu.VMEM((2, chips, share, features), BF16),
            pltpu.VMEM((chips, share, features), BF16),
            pltpu.VMEM((chips, share, features), BF16),
            pltpu.VMEM((chips, share, features), BF16),
            pltpu.VMEM((LANES, taps_n * LANES), F32),
            pltpu.VMEM((channels, 128), F32),
            pltpu.VMEM((devices, channels, 128), F32),
            pltpu.SemaphoreType.DMA((6,)),
            pltpu.SemaphoreType.DMA((blocks,)),
            pltpu.SemaphoreType.DMA((2, blocks)),
            pltpu.SemaphoreType.DMA((2, blocks)),
            pltpu.SemaphoreType.DMA((2, blocks)),
            pltpu.SemaphoreType.DMA((2, blocks)),
            pltpu.SemaphoreType.DMA((blocks,)),
            pltpu.SemaphoreType.DMA((blocks,)),
            pltpu.SemaphoreType.DMA((chips,)),
            pltpu.SemaphoreType.DMA((chips,)),
            pltpu.SemaphoreType.DMA((devices,)),
            pltpu.SemaphoreType.DMA((devices,)),
        ],
        compiler_params=pltpu.CompilerParams(
            collective_id=0, has_side_effects=True, vmem_limit_bytes=63 * 1024 * 1024
        ),
    )(
        columns_in, cotangent, conv_weight, mix_weight, neighbours.T,
        rotations.reshape(1, tile), pentagons.reshape(1, tile),
    )
    grad_conv = conv.reshape(channels, 128 // channels, channels)[:, :taps_n].transpose(1, 2, 0)
    return grad_input, grad_mix, grad_conv


def solution(mesh):
    return jax.shard_map(
        shards,
        mesh=mesh,
        in_specs=(
            P(("group", "space"), None),
            P(("group", "space"), None),
            P(),
            P(),
            P("space", None),
            P("space"),
            P("space"),
        ),
        out_specs=(P(("group", "space"), None), P("space", "group"), P("group", None, None)),
        check_vma=False,
    )
```

time: 71.9 us -> 56.8 us (0.79)
  Pallas kernels: 62.6 us -> 51 us
  other arithmetic: 3.23 us -> 0 us
    pallas_call x1, Pallas kernels: 62.6 us -> 51 us  [shards(): pl.pallas_call(functools.partial(kernel, devices), out_shape=(jax.ShapeDt...]
    select_n x3 -> x0, other arithmetic: 2.53 us -> none  [the longest x2 1.82 us: shards(): index_t = jnp.where((slot == 6) & (pentagons[None, :] != 0), -1, source)]
    unnamed x8 -> x2, local copies, waits for them, and re-layouts: 4.32 us -> 3.54 us
where the time goes in v2:
time: 56.8 us; the launch traced here: 56.6 us
  Pallas kernels  51 us (90%)
  local copies, waits for them, and re-layouts  4.96 us (9%)
  between operations  0.64 us (1%)
    pallas_call x1, Pallas kernels, shards(): pl.pallas_call(functools.partial(kernel, devices), out_shape=(jax.ShapeDt...  51 us
    unnamed x2, local copies, waits for them, and re-layouts  3.54 us

profile of v2, /device:TPU:0, one launch (start us, length us, event | category | flops | bytes accessed | tf_op | source)
XLA Modules:
  0.0 56.6 jit_solution(12488883563742348242)
XLA Ops:
  0.6 51.0 %shard_map.94 = (bf16[256,1024]{1,0:T(8,128)(2,1)}, f32[64,1024]{1,0:T(8,128)}, f32[16,128]{1,0:T(8,128)}) custom-call(bf16[256,1024]{1,0:T(8,128)(2,1)} %x_ref.1, bf16[256,1024]{1,0:T(8,128)(2,1)} %cot_hbm.1, bf16[7,16,16]{2,1,0:T(8,128)(2,1)} %conv_hbm.1, bf16[1024,1024]{1,0:T(8,128)(2,1)} %mix_hbm.1, s32[7,256]{1,0:T(8,128)} %bitcast.7, ...), custom_call_target="tpu_custom_call" | custom-call | tf_op jit(solution)/shard_map/pallas_call | solution.py:299
  51.6 0.8 %copy.11 = f32[16,128]{0,1:T(8,128)S(1)} copy(f32[16,128]{1,0:T(8,128)} %get-tuple-element.8) | data formatting | bytes 16384 | tf_op jit(solution)/shard_map/reshape | solution.py:355
  52.4 0.6 %slice_bitcast_fusion = f32[7,16,16]{2,1,0:T(8,128)} fusion(f32[16,8,16]{0,2,1:T(8,128)S(1)} %bitcast.6), kind=kLoop, calls=%fused_computation | loop fusion | bytes 14336 | tf_op jit(solution)/shard_map/transpose | solution.py:355
  53.1 1.9 %copy.14 = bf16[256,1024]{1,0:T(8,128)(2,1)} copy(bf16[256,1024]{1,0:T(8,128)(2,1)} %get-tuple-element.12) | data formatting | bytes 1048576
  54.9 1.7 %copy.15 = f32[64,1024]{1,0:T(8,128)} copy(f32[64,1024]{1,0:T(8,128)} %get-tuple-element.13) | data formatting | bytes 524288

commit v3 on v2

--- a/solution.py
+++ b/solution.py
@@ -34,9 +34,9 @@
     grad_ref, gmix_ref, gconv_ref,
     cot_ref, conv_ref, mix_ref, near_ref, rot_ref, pent_ref, index_pad,
     ext, hot, hot_t, wide, wide_t, ups, taps, gpre, terms, spread_mid, edges, edges_in,
-    part, part_in, summed, summed_in, conv_acc, conv_own, conv_in,
+    part, part_in, summed, pair_in, paired, summed_in, conv_acc, conv_own, conv_in,
     load_sem, mid_sem, halo_send, halo_recv, edge_send, edge_recv, core_send, core_recv,
-    chip_send, chip_recv, conv_send, conv_recv,
+    pair_send, pair_recv, chip_send, chip_recv, conv_send, conv_recv,
 ):
     tile, features = x_ref.shape
     taps_n, channels, _ = conv_ref.shape
@@ -166,23 +166,42 @@
             part.at[1 - core, at], part_in.at[at], core_send.at[k], core_recv.at[k], twin
         )
 
+    half = owners // 4
+    pairs = chips // 2
+    parity = lax.rem(chip, 2)
+    pair = chip // 2
+    mate = (chip + 1 - 2 * parity) * 2 + core
+
+    def pair_copy(k):
+        at = pl.ds(k * half, half)
+        return remote(
+            summed.at[1 - parity, at], pair_in.at[at], pair_send.at[k], pair_recv.at[k], mate
+        )
+
     def chip_copy(target, d):
         return remote(
-            summed.at[target], summed_in.at[d], chip_send.at[d], chip_recv.at[d],
-            target * 2 + core,
+            paired.at[target], summed_in.at[d], chip_send.at[d], chip_recv.at[d],
+            (target * 2 + parity) * 2 + core,
         )
 
     def pass_on(k):
         core_copy(k).wait()
-
-        @pl.loop(0, owners // 2)
-        def _(n):
+        for n in range(owners // 2):
             h = k * (owners // 2) + n
-            summed[h] = (part[core, h].astype(F32) + part_in[h].astype(F32)).astype(BF16)
-
-            @pl.when(h != chip)
+            summed[n % 2, k * half + n // 2] = (
+                part[core, h].astype(F32) + part_in[h].astype(F32)
+            ).astype(BF16)
+        pair_copy(k).start()
+
+    def send_far(k):
+        pair_copy(k).wait()
+        for n in range(half):
+            q = k * half + n
+            paired[q] = (summed[parity, q].astype(F32) + pair_in[q].astype(F32)).astype(BF16)
+
+            @pl.when(q != pair)
             def _():
-                chip_copy(h, lax.rem(h - chip + chips, chips)).start()
+                chip_copy(q, lax.rem(q - pair + pairs, pairs)).start()
 
     @pl.loop(0, blocks)
     def _(i):
@@ -220,9 +239,16 @@
         edges[1, k] = dot(hot_t[ROW + tile :, :], terms[...]).astype(BF16)
         edge_next(k).start()
         pass_on(k)
+
+        @pl.when(i > 0)
+        def _():
+            send_far(block_at(i - 1, me))
+
         own = dot(g, wide_t[:, 0:LANES]) + cot_ref[:, cols].astype(F32)
         spread_mid[k] = own + dot(hot_t[ROW : ROW + tile, :], terms[...])
         conv_acc[...] += dot(g, taps[k], ((0,), (0,)))
+
+    send_far(block_at(blocks - 1, me))
 
     rows_same = lax.broadcasted_iota(jnp.int32, (LANES, LANES), 0) // channels
     cols_same = lax.broadcasted_iota(jnp.int32, (LANES, LANES), 1) // channels
@@ -269,11 +295,11 @@
         1.0 / (devices * tile * (features // channels)) ** 0.5
     )
 
-    gmix_ref[...] = part[core, chip].astype(F32) + part_in[chip].astype(F32)
-
-    @pl.loop(1, chips)
+    gmix_ref[...] = summed[parity, pair].astype(F32) + pair_in[pair].astype(F32)
+
+    @pl.loop(1, pairs)
     def _(d):
-        chip_copy(lax.rem(chip + d, chips), d).wait()
+        chip_copy(lax.rem(pair + d, pairs), d).wait()
         gmix_ref[...] += summed_in[d].astype(F32)
 
     gmix_ref[...] = gmix_ref[...] * (1.0 / (devices * tile) ** 0.5)
@@ -327,8 +353,10 @@
             pltpu.VMEM((2, blocks, ROW, LANES), BF16),
             pltpu.VMEM((2, chips, share, features), BF16),
             pltpu.VMEM((chips, share, features), BF16),
-            pltpu.VMEM((chips, share, features), BF16),
-            pltpu.VMEM((chips, share, features), BF16),
+            pltpu.VMEM((2, chips // 2, share, features), BF16),
+            pltpu.VMEM((chips // 2, share, features), BF16),
+            pltpu.VMEM((chips // 2, share, features), BF16),
+            pltpu.VMEM((chips // 2, share, features), BF16),
             pltpu.VMEM((LANES, taps_n * LANES), F32),
             pltpu.VMEM((channels, 128), F32),
             pltpu.VMEM((devices, channels, 128), F32),
@@ -340,8 +368,10 @@
             pltpu.SemaphoreType.DMA((2, blocks)),
             pltpu.SemaphoreType.DMA((blocks,)),
             pltpu.SemaphoreType.DMA((blocks,)),
-            pltpu.SemaphoreType.DMA((chips,)),
-            pltpu.SemaphoreType.DMA((chips,)),
+            pltpu.SemaphoreType.DMA((blocks,)),
+            pltpu.SemaphoreType.DMA((blocks,)),
+            pltpu.SemaphoreType.DMA((chips // 2,)),
+            pltpu.SemaphoreType.DMA((chips // 2,)),
             pltpu.SemaphoreType.DMA((devices,)),
             pltpu.SemaphoreType.DMA((devices,)),
         ],

time: 56.8 us -> 55.5 us (0.977)
  Pallas kernels: 51 us -> 49.7 us
    pallas_call x1, Pallas kernels: 51 us -> 49.7 us  [shards(): pl.pallas_call(functools.partial(kernel, devices), out_shape=(jax.ShapeDt...]
where the time goes in v3:
time: 55.5 us; the launch traced here: 55.3 us
  Pallas kernels  49.7 us (90%)
  local copies, waits for them, and re-layouts  4.96 us (9%)
  between operations  0.64 us (1%)
    pallas_call x1, Pallas kernels, shards(): pl.pallas_call(functools.partial(kernel, devices), out_shape=(jax.ShapeDt...  49.7 us
    unnamed x2, local copies, waits for them, and re-layouts  3.54 us

profile of v3, /device:TPU:0, one launch (start us, length us, event | category | flops | bytes accessed | tf_op | source)
XLA Modules:
  0.0 55.3 jit_solution(13450632200057395379)
XLA Ops:
  0.6 49.7 %shard_map.94 = (bf16[256,1024]{1,0:T(8,128)(2,1)}, f32[64,1024]{1,0:T(8,128)}, f32[16,128]{1,0:T(8,128)}) custom-call(bf16[256,1024]{1,0:T(8,128)(2,1)} %x_ref.1, bf16[256,1024]{1,0:T(8,128)(2,1)} %cot_hbm.1, bf16[7,16,16]{2,1,0:T(8,128)(2,1)} %conv_hbm.1, bf16[1024,1024]{1,0:T(8,128)(2,1)} %mix_hbm.1, s32[7,256]{1,0:T(8,128)} %bitcast.7, ...), custom_call_target="tpu_custom_call" | custom-call | tf_op jit(solution)/shard_map/pallas_call | solution.py:325
  50.3 0.8 %copy.11 = f32[16,128]{0,1:T(8,128)S(1)} copy(f32[16,128]{1,0:T(8,128)} %get-tuple-element.8) | data formatting | bytes 16384 | tf_op jit(solution)/shard_map/reshape | solution.py:385
  51.1 0.6 %slice_bitcast_fusion = f32[7,16,16]{2,1,0:T(8,128)} fusion(f32[16,8,16]{0,2,1:T(8,128)S(1)} %bitcast.6), kind=kLoop, calls=%fused_computation | loop fusion | bytes 14336 | tf_op jit(solution)/shard_map/transpose | solution.py:385
  51.7 1.9 %copy.14 = bf16[256,1024]{1,0:T(8,128)(2,1)} copy(bf16[256,1024]{1,0:T(8,128)(2,1)} %get-tuple-element.12) | data formatting | bytes 1048576
  53.6 1.7 %copy.15 = f32[64,1024]{1,0:T(8,128)} copy(f32[64,1024]{1,0:T(8,128)} %get-tuple-element.13) | data formatting | bytes 524288
